TPU v7x, 32 devices: a whole 2x2x4 slice. The times are simulated.
32 devices in a mesh: parts: 32 (over z, y, x, core).
Axes of the slice: x: 2, y: 2, z: 4, core: 2. Of those that a mesh axis runs over, the one named last changes fastest.
Arguments:
- a_cols: int32 [1024, 7], replicated, may hold values from 0 to 1023, as said below
- p_col: int32 [1024], replicated, may hold values from 0 to 63, as said below
- coarse_cols: int32 [64, 14], replicated, may hold values from 0 to 63, as said below
- a_vals: bfloat16 [1024, 7, 192, 192], P('parts'), may hold values from -0.15625 to 0.15625
- p_vals: bfloat16 [1024, 192, 192], P('parts'), may hold values from -0.5 to 0.5
Outputs:
- coarse: float32 [64, 14, 192, 192], P('parts')
Inputs may be any that keep to these rules, and one draw needn't show every extreme that they name: `a_cols`: regions are numbered 0 to 31; fine row i lies in region g = i // 32 with local index l = i % 32; o is the list 0, 1, -1, 4, -4, 16, -16 and region g + o(s) is taken cyclically. Slot 0 of row i holds i. For l < 6, slot l + 1 holds the row of region g + o(l + 1) whose local index is q - 1, where q is the slot whose offset is the negative of o(l + 1), and the other slots hold rows of region g with local index 6 or more. For l >= 6 slots 1 to 6 hold rows of region g. For fine row i of region g with local index l: if l < 6, p_col[i] is a coarse row of region g + o(l + 1), else of region g; coarse row r belongs to region r // 2. `coarse_cols`: row r of region g lists, in an order of its own, the 2 coarse rows of each of the regions g + o(s), s = 0 to 6.
All inputs are finite; a program needn't handle non-finite values.
Results may differ from a plain program's by a relative error of at most 0.0029.
Values may be sent and summed in bfloat16 or wider, within the bound.
A program may use at most 256 MiB of HBM per device.

v0:
```python
import jax
import jax.numpy as jnp
from jax import lax
from jax.sharding import PartitionSpec as P

OFFSETS = [0, 1, -1, 4, -4, 16, -16]
OPPOSITE = [0, 2, 1, 4, 3, 6, 5]


def shifted(value, axis, by):
    count = lax.axis_size(axis)
    return lax.ppermute(value, axis, [(i, (i + by) % count) for i in range(count)])


def spread(coarse_ids, targets, galerkin, listed, first_coarse, form):
    coarse_count = listed.shape[0]
    local_coarse = coarse_ids - first_coarse
    hit_row = local_coarse[:, None] == jnp.arange(coarse_count, dtype=jnp.int32)[None, :]
    equal_slots = listed[None, None, :, :] == targets[:, :, None, None]
    first_slot = equal_slots & (jnp.cumsum(equal_slots.astype(jnp.int32), axis=3) == 1)
    weights = (first_slot & hit_row[:, None, :, None]).astype(jnp.float32)
    return jnp.einsum(form, weights, galerkin, precision=lax.Precision.HIGHEST)


def per_device(a_cols, p_col, coarse_cols, a_vals, p_vals):
    row_count = a_vals.shape[0]
    region_count = lax.axis_size("parts")
    region_id = lax.axis_index("parts")
    coarse_count = coarse_cols.shape[0] // region_count
    first_row = region_id * row_count
    first_coarse = region_id * coarse_count
    face_blocks = []
    for face_id in range(1, 7):
        face_blocks.append(shifted(p_vals[face_id - 1], "parts", OFFSETS[face_id]))
    prolong_pool = jnp.concatenate([p_vals, jnp.stack(face_blocks)], axis=0)
    columns = lax.dynamic_slice_in_dim(a_cols, first_row, row_count, 0)
    face_index = row_count + jnp.array(OPPOSITE, dtype=jnp.int32) - 1
    outside = columns // row_count != region_id
    pool_index = jnp.where(outside, face_index[None, :], columns - first_row)
    gathered = prolong_pool[pool_index]
    products = jnp.einsum(
        "ikab,ikbc->ikac", a_vals, gathered, preferred_element_type=jnp.float32
    ).astype(jnp.bfloat16)
    targets = p_col[columns]
    own_coarse = lax.dynamic_slice_in_dim(p_col, first_row, row_count, 0)
    listed = lax.dynamic_slice_in_dim(coarse_cols, first_coarse, coarse_count, 0)
    inner_terms = jnp.einsum(
        "iba,ikbc->iakc", p_vals[6:], products[6:], preferred_element_type=jnp.float32
    )
    accumulated = spread(
        own_coarse[6:], targets[6:], inner_terms, listed, first_coarse, "ikmc,iakb->mcab"
    )
    received = []
    sender_ids = []
    sender_targets = []
    face_terms = jnp.einsum(
        "iba,ikbc->iakc", p_vals[:6], products[:6], preferred_element_type=jnp.float32
    )
    for face_id in range(1, 7):
        received.append(shifted(face_terms[face_id - 1], "parts", OFFSETS[face_id]))
    for face_id in range(1, 7):
        sender = (region_id - OFFSETS[face_id]) % region_count
        sender_row = sender * row_count + face_id - 1
        sender_ids.append(p_col[sender_row])
        sender_targets.append(p_col[a_cols[sender_row]])
    form = "ikmc,iakb->mcab"
    accumulated = accumulated + spread(
        jnp.stack(sender_ids),
        jnp.stack(sender_targets),
        jnp.stack(received),
        listed,
        first_coarse,
        form,
    )
    return accumulated


def solution(mesh):
    placed = (P(), P(), P(), P("parts", None, None, None), P("parts", None, None))
    return jax.shard_map(
        per_device,
        mesh=mesh,
        in_specs=placed,
        out_specs=P("parts", None, None, None),
        check_vma=False,
    )
```

profile of v0, /device:TPU:0, one launch (start us, length us, event | category | flops | bytes accessed | tf_op | source)
XLA Modules:
  0.0 288.3 jit_solution(17692377658673620074)
XLA Ops:
  2.5 5.9 %collective-permute-start.1 = (bf16[192,192]{1,0:T(8,128)(2,1)}, bf16[192,192]{1,0:T(8,128)(2,1)}, u32[]{:S(2)}, u32[]{:S(2)}) collective-permute-start(bf16[192,192]{1,0:T(8,128)(2,1)} %get-tuple-element.21), channel_id=1, source_target_pairs={{0,31},{1,0},{2,1},{3,2},{4,3},{5,4},{6,5},{7,6},{8,7},{9,8},{10,9... | collective-permute-start | bytes 221192 | tf_op jit(solution)/shard_map/ppermute | solution.py:12
  8.4 4.7 %collective-permute-start.3 = (bf16[192,192]{1,0:T(8,128)(2,1)}, bf16[192,192]{1,0:T(8,128)(2,1)}, u32[]{:S(2)}, u32[]{:S(2)}) collective-permute-start(bf16[192,192]{1,0:T(8,128)(2,1)} %get-tuple-element.19), channel_id=1, source_target_pairs={{0,28},{1,29},{2,30},{3,31},{4,0},{5,1},{6,2},{7,3},{8,4},{9,5},{1... | collective-permute-start | bytes 221192 | tf_op jit(solution)/shard_map/ppermute | solution.py:12
  13.2 3.9 %constant_dynamic-update-slice_fusion = bf16[38,192,192]{2,1,0:T(8,128)(2,1)} fusion(bf16[32,192,192]{2,1,0:T(8,128)(2,1)} %param.10), kind=kLoop, calls=%fused_computation.61 | loop fusion | bytes 5505024
  27.4 4.7 %reduce_window_sum.23 = s32[6,7,2,14]{3,1,0,2:T(8,128)} reduce-window(s32[6,7,2,14]{3,1,0,2:T(8,128)S(1)} %compare_convert_fusion.1, s32[]{:T(128)} %constant.100.clone.1), window={size=1x1x1x14 pad=0_0x0_0x0_0x13_0}, to_apply=%region_1.2 | reduce-window | flops 15288 | bytes 9412 | tf_op jit(solution)/shard_map/jit(cumsum)/reduce_window_sum | solution.py:20
  32.1 3.9 %stack.76 = s32[6]{0:T(128)S(1)} concatenate(s32[1]{0:T(128)} %get-tuple-element.29, s32[1]{0:T(128)} %get-tuple-element.28, s32[1]{0:T(128)} %get-tuple-element.27, s32[1]{0:T(128)} %get-tuple-element.26, s32[1]{0:T(128)} %get-tuple-element.30, s32[1]{0:T(128)} %get-tuple-element.25), dimensions={0} | concatenate | bytes 48 | tf_op jit(solution)/shard_map/stack | solution.py:68
  36.7 3.0 %collective-permute-start.5 = (bf16[192,192]{1,0:T(8,128)(2,1)S(1)}, bf16[192,192]{1,0:T(8,128)(2,1)S(1)}, u32[]{:S(2)}, u32[]{:S(2)}) collective-permute-start(bf16[192,192]{1,0:T(8,128)(2,1)S(1)} %get-tuple-element.17), channel_id=1, source_target_pairs={{0,16},{1,17},{2,18},{3,19},{4,20},{5,21},{6,22},{7,23},{8,24},{9,... | collective-permute-start | bytes 221192 | tf_op jit(solution)/shard_map/ppermute | solution.py:12
  48.0 13.8 %gather_fusion.1 = bf16[224,192,192]{2,1,0:T(8,128)(2,1)} fusion(bf16[38,192,192]{2,1,0:T(8,128)(2,1)} %bitcast_dynamic-update-slice_fusion.6, s32[1024]{0:T(1024)S(1)} %pad_clamp_fusion.6), kind=kCustom, calls=%fused_computation.1 | custom fusion | bytes 33031040 | tf_op jit(solution)/shard_map/gather | solution.py:40
  61.8 24.8 %convolution_convert_fusion = bf16[32,7,192,192]{3,2,1,0:T(8,128)(2,1)} fusion(bf16[32,7,192,192]{3,2,1,0:T(8,128)(2,1)} %bitcast.131, bf16[32,7,192,192]{3,2,1,0:T(8,128)(2,1)} %param.9), kind=kOutput, calls=%fused_computation.14 | convolution fusion | flops 3179151360 | bytes 49545216 | tf_op jit(solution)/shard_map/ikab,ikbc->ikac/dot_general | solution.py:41
  86.6 3.4 %fusion.8 = f32[6,192,7,192]{1,3,2,0:T(8,128)S(1)} fusion(bf16[32,7,192,192]{3,2,1,0:T(8,128)(2,1)} %convolution_convert_fusion, bf16[32,192,192]{2,1,0:T(8,128)(2,1)S(1)} %copy-done.3), kind=kOutput, calls=%fused_computation.18 | convolution fusion | flops 594542592 | bytes 23298048 | tf_op jit(solution)/shard_map/iba,ikbc->iakc/dot_general | solution.py:56
  90.0 3.5 %slice_bitcast_fusion = (f32[192,7,192]{0,2,1:T(8,128)}, f32[192,7,192]{0,2,1:T(8,128)}, f32[192,7,192]{0,2,1:T(8,128)}, f32[192,7,192]{0,2,1:T(8,128)}, f32[192,7,192]{0,2,1:T(8,128)}, /*index=5*/f32[192,7,192]{0,2,1:T(8,128)}) fusion(f32[6,192,7,192]{1,3,2,0:T(8,128)S(1)} %fusion.8), kind=kLoop, calls=%fused_computation.21 | loop fusion | bytes 12386304 | tf_op jit(solution)/shard_map/squeeze | solution.py:60
  93.5 5.3 %collective-permute-start.7 = (f32[192,7,192]{0,2,1:T(8,128)}, f32[192,7,192]{0,2,1:T(8,128)}, u32[]{:S(2)}, u32[]{:S(2)}) collective-permute-start(f32[192,7,192]{0,2,1:T(8,128)} %get-tuple-element.15), channel_id=1, source_target_pairs={{0,31},{1,0},{2,1},{3,2},{4,3},{5,4},{6,5},{7,6},{8,7},{9,8},{10,9... | collective-permute-start | bytes 3096584 | tf_op jit(solution)/shard_map/ppermute | solution.py:12
  98.9 4.7 %collective-permute-start.9 = (f32[192,7,192]{0,2,1:T(8,128)}, f32[192,7,192]{0,2,1:T(8,128)}, u32[]{:S(2)}, u32[]{:S(2)}) collective-permute-start(f32[192,7,192]{0,2,1:T(8,128)} %get-tuple-element.13), channel_id=1, source_target_pairs={{0,28},{1,29},{2,30},{3,31},{4,0},{5,1},{6,2},{7,3},{8,4},{9,5},{1... | collective-permute-start | bytes 3096584 | tf_op jit(solution)/shard_map/ppermute | solution.py:12
  103.6 18.0 %fusion.4 = f32[26,7,192,192]{3,2,1,0:T(8,128)} fusion(bf16[32,7,192,192]{3,2,1,0:T(8,128)(2,1)} %convolution_convert_fusion, bf16[26,192,192,1]{2,1,3,0:T(8,128)(2,1)S(1)} %copy-done.4), kind=kOutput, calls=%fused_computation.12 | convolution fusion | flops 2576351232 | bytes 45268992 | tf_op jit(solution)/shard_map/iba,ikbc->iakc/dot_general | solution.py:47
  121.6 46.4 %copy.22 = f32[26,7,192,192]{2,0,1,3:T(8,128)} copy(f32[26,7,192,192]{3,2,1,0:T(8,128)} %fusion.4) | data formatting | bytes 53673984 | tf_op jit(solution)/shard_map/iba,ikbc->iakc/dot_general | solution.py:47
  168.0 26.4 %fusion = f32[2,14,192,192,1]{3,1,4,2,0:T(8,128)} fusion(f32[26,7,192,192]{2,0,1,3:T(8,128)} %copy.22, s32[26,7,2,14]{0,3,1,2:T(8,128)S(1)} %copy-done.6, s32[26,7]{0,1:T(8,128)S(1)} %copy-done.11, s32[2,14]{1,0:T(2,128)S(1)} %copy-done.13, pred[26,2]{0,1:T(4,128)(4,1)S(1)} %copy-done.15), kind=kOutput, calls=%fused_computation.8 | convolution fusion | flops 2254327808 | bytes 30987036 | tf_op jit(solution)/shard_map/ikmc,iakb->mcab/dot_general | solution.py:22
  194.5 2.9 %collective-permute-start.11 = (f32[192,7,192]{0,2,1:T(8,128)S(1)}, f32[192,7,192]{0,2,1:T(8,128)S(1)}, u32[]{:S(2)}, u32[]{:S(2)}) collective-permute-start(f32[192,7,192]{0,2,1:T(8,128)S(1)} %copy-done.5), channel_id=1, source_target_pairs={{0,16},{1,17},{2,18},{3,19},{4,20},{5,21},{6,22},{7,23},{8,24},{9,... | collective-permute-start | bytes 3096584 | tf_op jit(solution)/shard_map/ppermute | solution.py:12
  197.4 2.6 bitcast_dynamic-update-slice_fusion.5
  202.5 2.6 bitcast_dynamic-update-slice_fusion.3
  207.7 32.4 %collective-permute-done.10 = f32[192,7,192]{0,2,1:T(8,128)} collective-permute-done((f32[192,7,192]{0,2,1:T(8,128)}, f32[192,7,192]{0,2,1:T(8,128)}, u32[]{:S(2)}, u32[]{:S(2)}) %collective-permute-start.10) | collective-permute-done | bytes 1032224 | tf_op jit(solution)/shard_map/ppermute | solution.py:12
  240.2 2.6 bitcast_dynamic-update-slice_fusion.1
  242.7 17.1 %collective-permute-done.11 = f32[192,7,192]{0,2,1:T(8,128)S(1)} collective-permute-done((f32[192,7,192]{0,2,1:T(8,128)S(1)}, f32[192,7,192]{0,2,1:T(8,128)S(1)}, u32[]{:S(2)}, u32[]{:S(2)}) %collective-permute-start.11) | collective-permute-done | bytes 1032224 | tf_op jit(solution)/shard_map/ppermute | solution.py:12
  261.0 10.1 %copy.18 = f32[6,192,7,192]{3,2,0,1:T(8,128)} copy(f32[6,192,7,192]{1,3,2,0:T(8,128)} %bitcast_dynamic-update-slice_fusion) | data formatting | bytes 12386304 | tf_op jit(solution)/shard_map/stack | solution.py:70
  271.1 11.6 %bitcast_add_fusion = f32[2,14,192,192]{3,1,2,0:T(8,128)S(1)} fusion(f32[2,14,192,192,1]{3,1,4,2,0:T(8,128)} %fusion, f32[6,192,7,192]{3,2,0,1:T(8,128)} %copy.18, s32[6,7,2,14]{3,1,0,2:T(8,128)S(1)} %copy-done.7, s32[6,7]{1,0:T(8,128)S(1)} %copy-done.9, s32[2,14]{1,0:T(2,128)S(1)} %copy-done.13, pred[6,2]{0,1:T(4,128)(4,1)S(1)} %copy-done.16), kind=kOutput, calls=%fused_computation.17 | convolution fusion | flops 521261664 | bytes 14455684 | tf_op jit(solution)/shard_map/ikmc,iakb->mcab/dot_general | solution.py:22
  282.7 5.6 %copy.19 = f32[2,14,192,192]{3,2,1,0:T(8,128)} copy(f32[2,14,192,192]{3,1,2,0:T(8,128)S(1)} %bitcast_add_fusion) | data formatting | bytes 8257536 | tf_op jit(solution)/shard_map/add | solution.py:67
  (102 shorter events, 28.1 us)
Async XLA Ops:
  0.0 21.9 %copy-start = (s32[64,14]{0,1:T(8,128)S(1)}, s32[64,14]{0,1:T(8,128)}, u32[]{:S(2)}) copy-start(s32[64,14]{0,1:T(8,128)} %param.8) | copy-start | bytes 10756
  0.0 17.1 %copy-start.3 = (bf16[32,192,192]{2,1,0:T(8,128)(2,1)S(1)}, bf16[32,192,192]{2,1,0:T(8,128)(2,1)}, u32[]{:S(2)}) copy-start(bf16[32,192,192]{2,1,0:T(8,128)(2,1)} %param.10) | copy-start | bytes 7077892
  2.0 34.6 %collective-permute-start = (bf16[192,192]{1,0:T(8,128)(2,1)}, bf16[192,192]{1,0:T(8,128)(2,1)}, u32[]{:S(2)}, u32[]{:S(2)}) collective-permute-start(bf16[192,192]{1,0:T(8,128)(2,1)} %get-tuple-element.22), channel_id=1, source_target_pairs={{0,1},{1,2},{2,3},{3,4},{4,5},{5,6},{6,7},{7,8},{8,9},{9,10},{10,1... | collective-permute-start | bytes 221192 | tf_op jit(solution)/shard_map/ppermute | solution.py:12
  2.5 38.7 %collective-permute-start.1 = (bf16[192,192]{1,0:T(8,128)(2,1)}, bf16[192,192]{1,0:T(8,128)(2,1)}, u32[]{:S(2)}, u32[]{:S(2)}) collective-permute-start(bf16[192,192]{1,0:T(8,128)(2,1)} %get-tuple-element.21), channel_id=1, source_target_pairs={{0,31},{1,0},{2,1},{3,2},{4,3},{5,4},{6,5},{7,6},{8,7},{9,8},{10,9... | collective-permute-start | bytes 221192 | tf_op jit(solution)/shard_map/ppermute | solution.py:12
  8.4 34.3 %collective-permute-start.2 = (bf16[192,192]{1,0:T(8,128)(2,1)}, bf16[192,192]{1,0:T(8,128)(2,1)}, u32[]{:S(2)}, u32[]{:S(2)}) collective-permute-start(bf16[192,192]{1,0:T(8,128)(2,1)} %get-tuple-element.20), channel_id=1, source_target_pairs={{0,4},{1,5},{2,6},{3,7},{4,8},{5,9},{6,10},{7,11},{8,12},{9,13},{1... | collective-permute-start | bytes 221192 | tf_op jit(solution)/shard_map/ppermute | solution.py:12
  8.4 35.8 %collective-permute-start.3 = (bf16[192,192]{1,0:T(8,128)(2,1)}, bf16[192,192]{1,0:T(8,128)(2,1)}, u32[]{:S(2)}, u32[]{:S(2)}) collective-permute-start(bf16[192,192]{1,0:T(8,128)(2,1)} %get-tuple-element.19), channel_id=1, source_target_pairs={{0,28},{1,29},{2,30},{3,31},{4,0},{5,1},{6,2},{7,3},{8,4},{9,5},{1... | collective-permute-start | bytes 221192 | tf_op jit(solution)/shard_map/ppermute | solution.py:12
  13.1 32.7 %collective-permute-start.4 = (bf16[192,192]{1,0:T(8,128)(2,1)S(1)}, bf16[192,192]{1,0:T(8,128)(2,1)}, u32[]{:S(2)}, u32[]{:S(2)}) collective-permute-start(bf16[192,192]{1,0:T(8,128)(2,1)S(1)} %get-tuple-element.18), channel_id=1, source_target_pairs={{0,16},{1,17},{2,18},{3,19},{4,20},{5,21},{6,22},{7,23},{8,24},{9,... | collective-permute-start | bytes 221192 | tf_op jit(solution)/shard_map/ppermute | solution.py:12
  21.9 39.9 %copy-start.10 = (s32[26,7]{0,1:T(8,128)}, s32[26,7]{0,1:T(8,128)S(1)}, u32[]{:S(2)}) copy-start(s32[26,7]{0,1:T(8,128)S(1)} %copy.14) | copy-start | bytes 2188
  22.1 39.7 %copy-start.12 = (s32[2,14]{1,0:T(2,128)}, s32[2,14]{1,0:T(2,128)S(1)}, u32[]{:S(2)}) copy-start(s32[2,14]{1,0:T(2,128)S(1)} %copy.12) | copy-start | bytes 340
  36.7 10.7 %collective-permute-start.5 = (bf16[192,192]{1,0:T(8,128)(2,1)S(1)}, bf16[192,192]{1,0:T(8,128)(2,1)S(1)}, u32[]{:S(2)}, u32[]{:S(2)}) collective-permute-start(bf16[192,192]{1,0:T(8,128)(2,1)S(1)} %get-tuple-element.17), channel_id=1, source_target_pairs={{0,16},{1,17},{2,18},{3,19},{4,20},{5,21},{6,22},{7,23},{8,24},{9,... | collective-permute-start | bytes 221192 | tf_op jit(solution)/shard_map/ppermute | solution.py:12
  90.0 13.6 %copy-start.4 = (bf16[26,192,192,1]{2,1,3,0:T(8,128)(2,1)S(1)}, bf16[26,192,192,1]{2,1,3,0:T(8,128)(2,1)}, u32[]{:S(2)}) copy-start(bf16[26,192,192,1]{2,1,3,0:T(8,128)(2,1)} %fusion.50) | copy-start | bytes 5750788
  93.5 100.9 %collective-permute-start.6 = (f32[192,7,192]{0,2,1:T(8,128)}, f32[192,7,192]{0,2,1:T(8,128)}, u32[]{:S(2)}, u32[]{:S(2)}) collective-permute-start(f32[192,7,192]{0,2,1:T(8,128)} %get-tuple-element.16), channel_id=1, source_target_pairs={{0,1},{1,2},{2,3},{3,4},{4,5},{5,6},{6,7},{7,8},{8,9},{9,10},{10,1... | collective-permute-start | bytes 3096584 | tf_op jit(solution)/shard_map/ppermute | solution.py:12
  93.5 106.4 %collective-permute-start.7 = (f32[192,7,192]{0,2,1:T(8,128)}, f32[192,7,192]{0,2,1:T(8,128)}, u32[]{:S(2)}, u32[]{:S(2)}) collective-permute-start(f32[192,7,192]{0,2,1:T(8,128)} %get-tuple-element.15), channel_id=1, source_target_pairs={{0,31},{1,0},{2,1},{3,2},{4,3},{5,4},{6,5},{7,6},{8,7},{9,8},{10,9... | collective-permute-start | bytes 3096584 | tf_op jit(solution)/shard_map/ppermute | solution.py:12
  98.9 103.6 %collective-permute-start.8 = (f32[192,7,192]{0,2,1:T(8,128)}, f32[192,7,192]{0,2,1:T(8,128)}, u32[]{:S(2)}, u32[]{:S(2)}) collective-permute-start(f32[192,7,192]{0,2,1:T(8,128)} %get-tuple-element.14), channel_id=1, source_target_pairs={{0,4},{1,5},{2,6},{3,7},{4,8},{5,9},{6,10},{7,11},{8,12},{9,13},{1... | collective-permute-start | bytes 3096584 | tf_op jit(solution)/shard_map/ppermute | solution.py:12
  98.9 106.3 %collective-permute-start.9 = (f32[192,7,192]{0,2,1:T(8,128)}, f32[192,7,192]{0,2,1:T(8,128)}, u32[]{:S(2)}, u32[]{:S(2)}) collective-permute-start(f32[192,7,192]{0,2,1:T(8,128)} %get-tuple-element.13), channel_id=1, source_target_pairs={{0,28},{1,29},{2,30},{3,31},{4,0},{5,1},{6,2},{7,3},{8,4},{9,5},{1... | collective-permute-start | bytes 3096584 | tf_op jit(solution)/shard_map/ppermute | solution.py:12
  103.6 136.6 %collective-permute-start.10 = (f32[192,7,192]{0,2,1:T(8,128)}, f32[192,7,192]{0,2,1:T(8,128)}, u32[]{:S(2)}, u32[]{:S(2)}) collective-permute-start(f32[192,7,192]{0,2,1:T(8,128)} %get-tuple-element.12), channel_id=1, source_target_pairs={{0,16},{1,17},{2,18},{3,19},{4,20},{5,21},{6,22},{7,23},{8,24},{9,... | collective-permute-start | bytes 3096584 | tf_op jit(solution)/shard_map/ppermute | solution.py:12
  121.6 46.4 %copy-start.6 = (s32[26,7,2,14]{0,3,1,2:T(8,128)S(1)}, s32[26,7,2,14]{0,3,1,2:T(8,128)}, u32[]{:S(2)}) copy-start(s32[26,7,2,14]{0,3,1,2:T(8,128)} %reduce_window_sum.22) | copy-start | bytes 61156
  121.6 46.4 %copy-start.11 = (s32[26,7]{0,1:T(8,128)S(1)}, s32[26,7]{0,1:T(8,128)}, u32[]{:S(2)}) copy-start(s32[26,7]{0,1:T(8,128)} %copy-done.10) | copy-start | bytes 2188
  121.6 46.4 %copy-start.13 = (s32[2,14]{1,0:T(2,128)S(1)}, s32[2,14]{1,0:T(2,128)}, u32[]{:S(2)}) copy-start(s32[2,14]{1,0:T(2,128)} %copy-done.12) | copy-start | bytes 340
  121.6 46.4 %copy-start.15 = (pred[26,2]{0,1:T(4,128)(4,1)S(1)}, pred[26,2]{0,1:T(4,128)(4,1)}, u32[]{:S(2)}) copy-start(pred[26,2]{0,1:T(4,128)(4,1)} %iota_compare_fusion.1) | copy-start | bytes 160
  168.0 26.5 %copy-start.5 = (f32[192,7,192]{0,2,1:T(8,128)S(1)}, f32[192,7,192]{0,2,1:T(8,128)}, u32[]{:S(2)}) copy-start(f32[192,7,192]{0,2,1:T(8,128)} %get-tuple-element.11) | copy-start | bytes 3096580
  194.5 65.3 %collective-permute-start.11 = (f32[192,7,192]{0,2,1:T(8,128)S(1)}, f32[192,7,192]{0,2,1:T(8,128)S(1)}, u32[]{:S(2)}, u32[]{:S(2)}) collective-permute-start(f32[192,7,192]{0,2,1:T(8,128)S(1)} %copy-done.5), channel_id=1, source_target_pairs={{0,16},{1,17},{2,18},{3,19},{4,20},{5,21},{6,22},{7,23},{8,24},{9,... | collective-permute-start | bytes 3096584 | tf_op jit(solution)/shard_map/ppermute | solution.py:12
  261.0 10.1 %copy-start.16 = (pred[6,2]{0,1:T(4,128)(4,1)S(1)}, pred[6,2]{0,1:T(4,128)(4,1)}, u32[]{:S(2)}) copy-start(pred[6,2]{0,1:T(4,128)(4,1)} %iota_compare_fusion) | copy-start | bytes 40
  271.1 17.3 %copy-start.1 = (s32[64,14]{0,1:T(8,128)S(1)}, s32[64,14]{0,1:T(8,128)}, u32[]{:S(2)}) copy-start(s32[64,14]{0,1:T(8,128)} %param.8) | copy-start | bytes 10756
  (6 other events, 47.4 us)
where the time goes:
time: 290 us; the launch traced here: 288 us
  local copies, waits for them, and re-layouts  120 us (41%)
  matrix products  84.2 us (29%)
  waiting for transfers between devices  49.5 us (17%)
  starting transfers between devices  27.1 us (9%)
  other arithmetic  6.89 us (2%)
    ppermute x12, waiting for transfers between devices, shifted(): lax.ppermute(value, axis, [(i, (i + by) % count) for i in range(count)])  49.5 us
    dot_general x2, local copies, waits for them, and re-layouts, per_device(): jnp.einsum('iba,ikbc->iakc', p_vals[6:], products[6:], preferred_element_...  48 us
    dot_general x2, matrix products, spread(): return jnp.einsum(form, weights, galerkin, precision=lax.Precision.HIGHEST)  38.1 us
    ppermute x12, starting transfers between devices, shifted(): lax.ppermute(value, axis, [(i, (i + by) % count) for i in range(count)])  27.1 us
    dot_general x1, matrix products, per_device(): jnp.einsum('ikab,ikbc->ikac', a_vals, gathered, preferred_element_type=jn...  24.8 us
    unnamed x47, local copies, waits for them, and re-layouts  24.6 us
    dot_general x1, matrix products, per_device(): jnp.einsum('iba,ikbc->iakc', p_vals[6:], products[6:], preferred_element_...  18 us
    gather x1, local copies, waits for them, and re-layouts, per_device(): gathered = prolong_pool[pool_index]  13.8 us
  transfers between devices with their start and end apart: 12, of which 2 were waited for; matrix products, arithmetic and copies ran while one was open for 47% of the time, Pallas kernels for 0%

commit v1 on v0

v1 whole, which is shorter than its diff:
```python
import functools

import jax
import jax.numpy as jnp
from jax import lax
from jax.experimental import pallas as pl
from jax.experimental.pallas import tpu as pltpu
from jax.sharding import PartitionSpec as P

OFFSETS = [0, 1, -1, 4, -4, 16, -16]
OPPOSITE = [0, 2, 1, 4, 3, 6, 5]
KA = 7
FACES = 6
VMEM_LIMIT = 48 * 1024 * 1024
F32 = jnp.float32
BF16 = jnp.bfloat16


def dot(left, right):
    return jnp.dot(left, right, preferred_element_type=F32)


def pack(out_ref, at, blocks):
    for n, block in enumerate(blocks):
        out_ref[at + (n,)] = block[:, :128].astype(BF16)
    for n in range(2):
        rest = jnp.concatenate([blocks[2 * n][:, 128:], blocks[2 * n + 1][:, 128:]], axis=1)
        out_ref[at + (4 + n,)] = rest.astype(BF16)


def face_kernel(rows, row_count, earlier, cols_ref, pcol_ref, a_hbm, p_hbm, *rest):
    outs, (a_buf, p_buf, sums, a_sem, p_sem) = rest[earlier:-5], rest[-5:]
    region = lax.axis_index("parts")
    first_row = region * row_count
    copies = {}
    for n, row in enumerate(rows):
        for k in range(KA):
            copy = pltpu.make_async_copy(a_hbm.at[row, k], a_buf.at[n, k], a_sem.at[n, k])
            copy.start()
            if k == row + 1:
                copies[n, k] = (copy,)
                continue
            column = row if k == 0 else cols_ref[k, first_row + row] - first_row
            other = pltpu.make_async_copy(p_hbm.at[column], p_buf.at[n, k], p_sem.at[n, k])
            other.start()
            copies[n, k] = (copy, other)
    for n, row in enumerate(rows):
        for copy in copies[n, 0]:
            copy.wait()
        own_t = p_buf[n, 0].T
        diagonal = dot(own_t, dot(a_buf[n, 0], p_buf[n, 0]).astype(BF16))
        copies[n, row + 1][0].wait()
        half = dot(own_t, a_buf[n, row + 1])
        sums[...] = jnp.zeros_like(sums)
        for k in range(1, KA):
            if k == row + 1:
                continue
            for copy in copies[n, k]:
                copy.wait()
            side = pcol_ref[cols_ref[k, first_row + row]] % 2
            sums[side] += dot(a_buf[n, k], p_buf[n, k])
        inner = [dot(own_t, sums[c].astype(BF16)) for c in range(2)]
        out_ref, at = (outs[0], (n,)) if len(outs) == 1 else (outs[n], ())
        pack(out_ref, at, [diagonal, inner[0], inner[1], half])


def face_terms(rows, merged, a_t, p_col, a_vals, p_vals, earlier):
    row_count, _, width, _ = a_vals.shape
    one = jax.ShapeDtypeStruct((6, width, 128), BF16)
    both = jax.ShapeDtypeStruct((2, 6, width, 128), BF16)
    smem = pl.BlockSpec(memory_space=pltpu.SMEM)
    vmem = pl.BlockSpec(memory_space=pltpu.VMEM)
    anyw = pl.BlockSpec(memory_space=pl.ANY)
    return pl.pallas_call(
        functools.partial(face_kernel, rows, row_count, len(earlier)),
        out_shape=[both] if merged else [one, one],
        in_specs=[smem, smem, anyw, anyw] + [anyw] * len(earlier),
        out_specs=[vmem] * (1 if merged else 2),
        scratch_shapes=[
            pltpu.VMEM((2, KA, width, width), BF16),
            pltpu.VMEM((2, KA, width, width), BF16),
            pltpu.VMEM((2, width, width), F32),
            pltpu.SemaphoreType.DMA((2, KA)),
            pltpu.SemaphoreType.DMA((2, KA)),
        ],
        compiler_params=pltpu.CompilerParams(vmem_limit_bytes=VMEM_LIMIT),
        cost_estimate=pl.CostEstimate(flops=24 * 2 * width**3, bytes_accessed=5_000_000, transcendentals=0),
        name="faces_%d" % rows[0],
    )(a_t, p_col, a_vals, p_vals, *earlier)


def slot_of(listed_ref, coarse_row, local, column):
    slots = listed_ref.shape[0]
    found = jnp.int32(0)
    for m in reversed(range(slots)):
        found = jnp.where(listed_ref[m, coarse_row] == column, jnp.int32(m), found)
    return local * slots + found


def inner_kernel(row_count, coarse_count, pair, cols_ref, pcol_ref, listed_ref, a_ref, p_ref, out_ref, table):
    step = pl.program_id(0)
    region = lax.axis_index("parts")
    first_row = region * row_count
    first_coarse = region * coarse_count
    slots = listed_ref.shape[0]

    @pl.when(step == 0)
    def _():
        out_ref[...] = jnp.zeros_like(out_ref)
        for r in range(coarse_count):
            for m in reversed(range(slots)):
                table[r, listed_ref[m, first_coarse + r]] = r * slots + m

    for n in range(pair):
        row = FACES + step * pair + n
        local = pcol_ref[first_row + row] - first_coarse
        own_t = p_ref[row].T
        columns = [cols_ref[k, first_row + row] for k in range(KA)]
        products = [dot(a_ref[n, k], p_ref[columns[k] - first_row]).astype(BF16) for k in range(KA)]
        for k in range(KA):
            target = table[local, pcol_ref[columns[k]]]
            out_ref[target] += dot(own_t, products[k])


def inner_terms(a_t, p_col, listed_t, a_vals, p_vals, coarse_count):
    row_count, _, width, _ = a_vals.shape
    slots, coarse_all = listed_t.shape
    pair = 2
    smem = pl.BlockSpec(memory_space=pltpu.SMEM)
    return pl.pallas_call(
        functools.partial(inner_kernel, row_count, coarse_count, pair),
        out_shape=jax.ShapeDtypeStruct((coarse_count * slots, width, width), F32),
        grid=((row_count - FACES) // pair,),
        in_specs=[
            smem,
            smem,
            smem,
            pl.BlockSpec((pair, KA, width, width), lambda s: (s + FACES // pair, 0, 0, 0)),
            pl.BlockSpec((row_count, width, width), lambda s: (0, 0, 0), pipeline_mode=pl.Buffered(1)),
        ],
        out_specs=pl.BlockSpec((coarse_count * slots, width, width), lambda s: (0, 0, 0)),
        scratch_shapes=[pltpu.SMEM((coarse_count, coarse_all), jnp.int32)],
        compiler_params=pltpu.CompilerParams(vmem_limit_bytes=VMEM_LIMIT),
        cost_estimate=pl.CostEstimate(flops=364 * 4 * width**3, bytes_accessed=60_000_000, transcendentals=0),
        name="inner",
    )(a_t, p_col, listed_t, a_vals, p_vals)


def outer_kernel(row_count, coarse_count, regions, merged, pcol_ref, listed_ref, *rest):
    received, (p_ref, part_ref, out_ref) = rest[:-3], rest[-3:]
    region = lax.axis_index("parts")
    first_coarse = region * coarse_count
    out_ref[...] = part_ref[...]
    for face in range(FACES):
        ref, at = (received[4], (face - 4,)) if merged and face >= 4 else (received[face], ())
        sender = lax.rem(region - OFFSETS[face + 1] + regions, regions)
        coarse_row = pcol_ref[sender * row_count + face]
        local = coarse_row - first_coarse
        mine = OPPOSITE[face + 1] - 1
        own_row = region * coarse_count + local
        where = functools.partial(slot_of, listed_ref, own_row, local)
        for n, column in enumerate([coarse_row, sender * coarse_count, sender * coarse_count + 1]):
            target = where(column)
            out_ref[target, :, :128] += ref[at + (n,)].astype(F32)
            start = 64 * (n % 2)
            out_ref[target, :, 128:] += ref[at + (4 + n // 2,)][:, start : start + 64].astype(F32)
        block = dot(ref[at + (3,)], p_ref[mine, :128]) + dot(ref[at + (5,)][:, 64:], p_ref[mine, 128:])
        out_ref[where(pcol_ref[region * row_count + mine])] += block


def outer_terms(p_col, listed_t, received, p_vals, part, coarse_count, regions, merged):
    row_count, width, _ = p_vals.shape
    smem = pl.BlockSpec(memory_space=pltpu.SMEM)
    vmem = pl.BlockSpec(memory_space=pltpu.VMEM)
    faces = pl.BlockSpec((FACES, width, width), lambda s: (0, 0, 0))
    whole = pl.BlockSpec(part.shape, lambda s: (0, 0, 0))
    return pl.pallas_call(
        functools.partial(outer_kernel, row_count, coarse_count, regions, merged),
        out_shape=jax.ShapeDtypeStruct(part.shape, F32),
        grid=(1,),
        in_specs=[smem, smem] + [vmem] * len(received) + [faces, whole],
        out_specs=whole,
        compiler_params=pltpu.CompilerParams(vmem_limit_bytes=VMEM_LIMIT),
        name="outer",
    )(p_col, listed_t, *received, p_vals, part)


def per_device(a_cols, p_col, coarse_cols, a_vals, p_vals):
    regions = lax.axis_size("parts")
    coarse_count = coarse_cols.shape[0] // regions
    a_t = a_cols.T
    listed_t = coarse_cols.T
    merged = (OFFSETS[5] - OFFSETS[6]) % regions == 0
    sent = [None] * FACES
    outs = []
    for first in (4, 2, 0):
        outs = face_terms((first, first + 1), merged and first == 4, a_t, p_col, a_vals, p_vals, outs)
        for n, out in enumerate(outs):
            by = OFFSETS[first + n + 1]
            sent[first + n] = lax.ppermute(out, "parts", [(i, (i + by) % regions) for i in range(regions)])
    received = [value for value in sent if value is not None]
    part = inner_terms(a_t, p_col, listed_t, a_vals, p_vals, coarse_count)
    out = outer_terms(p_col, listed_t, received, p_vals, part, coarse_count, regions, merged)
    return out.reshape((coarse_count, -1) + out.shape[1:])


def solution(mesh):
    placed = (P(), P(), P(), P("parts", None, None, None), P("parts", None, None))
    return jax.shard_map(
        per_device,
        mesh=mesh,
        in_specs=placed,
        out_specs=P("parts", None, None, None),
        check_vma=False,
    )
```

time: 290 us -> 63.7 us (0.22)
  local copies, waits for them, and re-layouts: 120 us -> 3.34 us
  matrix products: 84.2 us -> 0 us
  waiting for transfers between devices: 49.5 us -> 0.01 us
  Pallas kernels: 0 us -> 45.4 us
  starting transfers between devices: 27.1 us -> 14.3 us
  other arithmetic: 6.89 us -> 0 us
    dot_general x5 -> x0, matrix products: 84.2 us -> none  [the longest x2 38.1 us: spread(): return jnp.einsum(form, weights, galerkin, precision=lax.Precision.HIGHEST)]
    ppermute x12 -> x5, waiting for transfers between devices: 49.5 us -> 0.01 us  [per_device(): lax.ppermute(out, 'parts', [(i, (i + by) % regions) for i in range(region...]
    dot_general x2 -> x0, local copies, waits for them, and re-layouts: 48 us -> none  [per_device(): jnp.einsum('iba,ikbc->iakc', p_vals[6:], products[6:], preferred_element_...]
    pallas_call x0 -> x5, Pallas kernels: none -> 45.4 us  [the longest x3 20.1 us: face_terms(): pl.pallas_call(functools.partial(face_kernel, rows, row_count, len(earlie...]
    unnamed x47 -> x10, local copies, waits for them, and re-layouts: 24.6 us -> 3.34 us
    gather x8 -> x0, local copies, waits for them, and re-layouts: 18.9 us -> none  [the longest x1 13.8 us: per_device(): gathered = prolong_pool[pool_index]]
    another operation x4 -> x0, local copies, waits for them, and re-layouts: 15.2 us -> none  [the longest x2 11.3 us: per_device(): jnp.stack(received)]
    ppermute x12 -> x5, starting transfers between devices: 27.1 us -> 14.3 us  [per_device(): lax.ppermute(out, 'parts', [(i, (i + by) % regions) for i in range(region...]
  transfers between devices with their start and end apart: 12 -> 5, of which waited for: 2 -> 0; matrix products, arithmetic and copies ran while one was open for 47% -> 0% of each run, Pallas kernels for 0% -> 52%
where the time goes in v1:
time: 63.7 us; the launch traced here: 63.1 us
  Pallas kernels  45.4 us (71%)
  starting transfers between devices  14.3 us (22%)
  local copies, waits for them, and re-layouts  3.34 us (5%)
    pallas_call x3, Pallas kernels, face_terms(): pl.pallas_call(functools.partial(face_kernel, rows, row_count, len(earlie...  20.1 us
    pallas_call x1, Pallas kernels, inner_terms(): pl.pallas_call(functools.partial(inner_kernel, row_count, coarse_count, p...  19.3 us
    ppermute x5, starting transfers between devices, per_device(): lax.ppermute(out, 'parts', [(i, (i + by) % regions) for i in range(region...  14.3 us
    pallas_call x1, Pallas kernels, outer_terms(): pl.pallas_call(functools.partial(outer_kernel, row_count, coarse_count, r...  6.08 us
    unnamed x10, local copies, waits for them, and re-layouts  3.34 us
  transfers between devices with their start and end apart: 5, of which 0 were waited for; matrix products, arithmetic and copies ran while one was open for 0% of the time, Pallas kernels for 52%

profile of v1, /device:TPU:0, one launch (start us, length us, event | category | flops | bytes accessed | tf_op | source)
XLA Modules:
  0.0 63.1 jit_solution(6017856588117706289)
XLA Ops:
  0.0 0.0 copy-start
  0.0 1.9 %copy-done = bf16[32,192,192]{2,1,0:T(8,128)(2,1)S(1)} copy-done((bf16[32,192,192]{2,1,0:T(8,128)(2,1)S(1)}, bf16[32,192,192]{2,1,0:T(8,128)(2,1)}, u32[]{:S(2)}) %copy-start) | copy-done | bytes 2359320
  1.9 0.8 %copy-done.2 = s32[1024,7]{0,1:T(8,128)S(1)} copy-done((s32[1024,7]{0,1:T(8,128)S(1)}, s32[1024,7]{0,1:T(8,128)}, u32[]{:S(2)}) %copy-start.2) | copy-done | bytes 28696
  2.6 0.0 copy-start.3
  2.7 0.7 %copy-done.3 = s32[1024]{0:T(1024)S(1)} copy-done((s32[1024]{0:T(1024)S(1)}, s32[1024]{0:T(1024)}, u32[]{:S(2)}) %copy-start.3) | copy-done | bytes 4120
  3.3 6.7 %faces_4.1.rest_0_ = bf16[2,6,192,128]{3,2,1,0:T(8,128)(2,1)S(1)} custom-call(s32[7,1024]{1,0:T(8,128)S(1)} %bitcast.3, s32[1024]{0:T(1024)S(1)} %copy-done.3, bf16[32,7,192,192]{3,2,1,0:T(8,128)(2,1)} %a_ref.1, bf16[32,192,192]{2,1,0:T(8,128)(2,1)S(1)} %copy-done), custom_call_target="tpu_custom_call" | custom-call | flops 339738624 | bytes 5000000 | tf_op jit(solution)/shard_map/faces_4/pallas_call | solution.py:74
  10.0 4.1 %collective-permute-start.4 = (bf16[2,6,192,128]{3,2,1,0:T(8,128)(2,1)S(1)}, bf16[2,6,192,128]{3,2,1,0:T(8,128)(2,1)S(1)}, u32[]{:S(2)}, u32[]{:S(2)}) collective-permute-start(bf16[2,6,192,128]{3,2,1,0:T(8,128)(2,1)S(1)} %faces_4.1.rest_0_), channel_id=1, source_target_pairs={{0,16},{1,17},{2,18},{3,19},{4,20},{5,21},{6,22},{7,23},{8,24},{9,... | collective-permute-start | bytes 1769480 | tf_op jit(solution)/shard_map/ppermute | solution.py:200
  14.1 6.7 %faces_2.1 = (bf16[6,192,128]{2,1,0:T(8,128)(2,1)S(1)}, bf16[6,192,128]{2,1,0:T(8,128)(2,1)S(1)}) custom-call(s32[7,1024]{1,0:T(8,128)S(1)} %bitcast.4, s32[1024]{0:T(1024)S(1)} %copy-done.3, bf16[32,7,192,192]{3,2,1,0:T(8,128)(2,1)} %a_ref.1, bf16[32,192,192]{2,1,0:T(8,128)(2,1)S(1)} %copy-done, bf16[2,6,192,128]{3,2,1,0:T(8,128)(2,1)S(1)} %faces_4.1.rest_0_), custom_call_target="tpu_custom_call" | custom-call | flops 339738624 | bytes 5000000 | tf_op jit(solution)/shard_map/faces_2/pallas_call | solution.py:74
  20.8 1.6 %collective-permute-start.2 = (bf16[6,192,128]{2,1,0:T(8,128)(2,1)S(1)}, bf16[6,192,128]{2,1,0:T(8,128)(2,1)S(1)}, u32[]{:S(2)}, u32[]{:S(2)}) collective-permute-start(bf16[6,192,128]{2,1,0:T(8,128)(2,1)S(1)} %get-tuple-element.9.rest_0_), channel_id=1, source_target_pairs={{0,4},{1,5},{2,6},{3,7},{4,8},{5,9},{6,10},{7,11},{8,12},{9,13},{1... | collective-permute-start | bytes 884744 | tf_op jit(solution)/shard_map/ppermute | solution.py:200
  22.4 0.0 copy-start.4
  22.4 3.2 %collective-permute-start.3 = (bf16[6,192,128]{2,1,0:T(8,128)(2,1)S(1)}, bf16[6,192,128]{2,1,0:T(8,128)(2,1)S(1)}, u32[]{:S(2)}, u32[]{:S(2)}) collective-permute-start(bf16[6,192,128]{2,1,0:T(8,128)(2,1)S(1)} %get-tuple-element.10.rest_1_), channel_id=1, source_target_pairs={{0,28},{1,29},{2,30},{3,31},{4,0},{5,1},{6,2},{7,3},{8,4},{9,5},{1... | collective-permute-start | bytes 884744 | tf_op jit(solution)/shard_map/ppermute | solution.py:200
  25.6 6.7 %faces_0.1 = (bf16[6,192,128]{2,1,0:T(8,128)(2,1)S(1)}, bf16[6,192,128]{2,1,0:T(8,128)(2,1)S(1)}) custom-call(s32[7,1024]{1,0:T(8,128)S(1)} %bitcast.5, s32[1024]{0:T(1024)S(1)} %copy-done.3, bf16[32,7,192,192]{3,2,1,0:T(8,128)(2,1)} %a_ref.1, bf16[32,192,192]{2,1,0:T(8,128)(2,1)S(1)} %copy-done, bf16[6,192,128]{2,1,0:T(8,128)(2,1)S(1)} %get-tuple-element.9.rest_0_, ...), custom_call_target="tpu_custom_call" | custom-call | flops 339738624 | bytes 5000000 | tf_op jit(solution)/shard_map/faces_0/pallas_call | solution.py:74
  32.3 0.1 collective-permute-start
  32.4 5.3 %collective-permute-start.1 = (bf16[6,192,128]{2,1,0:T(8,128)(2,1)S(1)}, bf16[6,192,128]{2,1,0:T(8,128)(2,1)S(1)}, u32[]{:S(2)}, u32[]{:S(2)}) collective-permute-start(bf16[6,192,128]{2,1,0:T(8,128)(2,1)S(1)} %get-tuple-element.12), channel_id=1, source_target_pairs={{0,31},{1,0},{2,1},{3,2},{4,3},{5,4},{6,5},{7,6},{8,7},{9,8},{10,9... | collective-permute-start | bytes 884744 | tf_op jit(solution)/shard_map/ppermute | solution.py:200
  37.7 0.0 copy-done.4
  37.7 0.0 copy-start.1
  37.7 19.3 %inner.1.rest_6_ = f32[28,192,192]{2,1,0:T(8,128)} custom-call(s32[7,1024]{1,0:T(8,128)S(1)} %bitcast.6, s32[1024]{0:T(1024)S(1)} %copy-done.3, s32[14,64]{1,0:T(8,128)S(1)} %bitcast.7, bf16[32,7,192,192]{3,2,1,0:T(8,128)(2,1)} %a_ref.1, bf16[32,192,192]{2,1,0:T(8,128)(2,1)S(1)} %copy-done), custom_call_target="tpu_custom_call" | custom-call | flops 10305404928 | bytes 60000000 | tf_op jit(solution)/shard_map/inner/pallas_call | solution.py:130
  57.0 0.0 collective-permute-done.2.rest_2_
  57.0 0.0 collective-permute-done.3.rest_3_
  57.0 0.0 collective-permute-done.rest_0_
  57.0 0.0 collective-permute-done.1.rest_1_
  57.0 0.0 collective-permute-done.4.rest_4_
  57.1 0.0 copy-done.1
  57.1 6.1 %outer.1 = f32[28,192,192]{2,1,0:T(8,128)} custom-call(s32[1024]{0:T(1024)S(1)} %copy-done.3, s32[14,64]{1,0:T(8,128)S(1)} %bitcast.8, bf16[6,192,128]{2,1,0:T(8,128)(2,1)S(1)} %collective-permute-done.rest_0_, bf16[6,192,128]{2,1,0:T(8,128)(2,1)S(1)} %collective-permute-done.1.rest_1_, bf16[6,192,128]{2,1,0:T(8,128)(2,1)S(1)} %collective-permute-done.2.rest_2_, ...), custom_call_target="tpu_custom_call" | custom-call | tf_op jit(solution)/shard_map/outer/pallas_call | solution.py:177
  (1 shorter events, 0.0 us)
Async XLA Ops:
  0.0 1.9 %copy-start = (bf16[32,192,192]{2,1,0:T(8,128)(2,1)S(1)}, bf16[32,192,192]{2,1,0:T(8,128)(2,1)}, u32[]{:S(2)}) copy-start(bf16[32,192,192]{2,1,0:T(8,128)(2,1)} %rest_5_.1) | copy-start | bytes 7077892
  1.9 0.8 %copy-start.2 = (s32[1024,7]{0,1:T(8,128)S(1)}, s32[1024,7]{0,1:T(8,128)}, u32[]{:S(2)}) copy-start(s32[1024,7]{0,1:T(8,128)} %param.5) | copy-start | bytes 86020
  2.6 0.7 %copy-start.3 = (s32[1024]{0:T(1024)S(1)}, s32[1024]{0:T(1024)}, u32[]{:S(2)}) copy-start(s32[1024]{0:T(1024)} %pcol_ref.9) | copy-start | bytes 12292
  10.0 47.0 %collective-permute-start.4 = (bf16[2,6,192,128]{3,2,1,0:T(8,128)(2,1)S(1)}, bf16[2,6,192,128]{3,2,1,0:T(8,128)(2,1)S(1)}, u32[]{:S(2)}, u32[]{:S(2)}) collective-permute-start(bf16[2,6,192,128]{3,2,1,0:T(8,128)(2,1)S(1)} %faces_4.1.rest_0_), channel_id=1, source_target_pairs={{0,16},{1,17},{2,18},{3,19},{4,20},{5,21},{6,22},{7,23},{8,24},{9,... | collective-permute-start | bytes 1769480 | tf_op jit(solution)/shard_map/ppermute | solution.py:200
  20.8 36.2 %collective-permute-start.2 = (bf16[6,192,128]{2,1,0:T(8,128)(2,1)S(1)}, bf16[6,192,128]{2,1,0:T(8,128)(2,1)S(1)}, u32[]{:S(2)}, u32[]{:S(2)}) collective-permute-start(bf16[6,192,128]{2,1,0:T(8,128)(2,1)S(1)} %get-tuple-element.9.rest_0_), channel_id=1, source_target_pairs={{0,4},{1,5},{2,6},{3,7},{4,8},{5,9},{6,10},{7,11},{8,12},{9,13},{1... | collective-permute-start | bytes 884744 | tf_op jit(solution)/shard_map/ppermute | solution.py:200
  22.4 15.3 %copy-start.4 = (s32[64,14]{0,1:T(8,128)S(1)}, s32[64,14]{0,1:T(8,128)}, u32[]{:S(2)}) copy-start(s32[64,14]{0,1:T(8,128)} %param.7) | copy-start | bytes 10756
  22.4 34.6 %collective-permute-start.3 = (bf16[6,192,128]{2,1,0:T(8,128)(2,1)S(1)}, bf16[6,192,128]{2,1,0:T(8,128)(2,1)S(1)}, u32[]{:S(2)}, u32[]{:S(2)}) collective-permute-start(bf16[6,192,128]{2,1,0:T(8,128)(2,1)S(1)} %get-tuple-element.10.rest_1_), channel_id=1, source_target_pairs={{0,28},{1,29},{2,30},{3,31},{4,0},{5,1},{6,2},{7,3},{8,4},{9,5},{1... | collective-permute-start | bytes 884744 | tf_op jit(solution)/shard_map/ppermute | solution.py:200
  32.3 24.7 %collective-permute-start = (bf16[6,192,128]{2,1,0:T(8,128)(2,1)S(1)}, bf16[6,192,128]{2,1,0:T(8,128)(2,1)S(1)}, u32[]{:S(2)}, u32[]{:S(2)}) collective-permute-start(bf16[6,192,128]{2,1,0:T(8,128)(2,1)S(1)} %get-tuple-element.11), channel_id=1, source_target_pairs={{0,1},{1,2},{2,3},{3,4},{4,5},{5,6},{6,7},{7,8},{8,9},{9,10},{10,1... | collective-permute-start | bytes 884744 | tf_op jit(solution)/shard_map/ppermute | solution.py:200
  32.4 24.7 %collective-permute-start.1 = (bf16[6,192,128]{2,1,0:T(8,128)(2,1)S(1)}, bf16[6,192,128]{2,1,0:T(8,128)(2,1)S(1)}, u32[]{:S(2)}, u32[]{:S(2)}) collective-permute-start(bf16[6,192,128]{2,1,0:T(8,128)(2,1)S(1)} %get-tuple-element.12), channel_id=1, source_target_pairs={{0,31},{1,0},{2,1},{3,2},{4,3},{5,4},{6,5},{7,6},{8,7},{9,8},{10,9... | collective-permute-start | bytes 884744 | tf_op jit(solution)/shard_map/ppermute | solution.py:200
  37.7 19.4 %copy-start.1 = (bf16[32,192,192]{2,1,0:T(8,128)(2,1)S(1)}, bf16[32,192,192]{2,1,0:T(8,128)(2,1)}, u32[]{:S(2)}) copy-start(bf16[32,192,192]{2,1,0:T(8,128)(2,1)} %rest_5_.1) | copy-start | bytes 7077892

commit v2 on v1

--- a/solution.py
+++ b/solution.py
@@ -29,7 +29,7 @@
 
 
 def face_kernel(rows, row_count, earlier, cols_ref, pcol_ref, a_hbm, p_hbm, *rest):
-    outs, (a_buf, p_buf, sums, a_sem, p_sem) = rest[earlier:-5], rest[-5:]
+    outs, (a_buf, p_buf, a_sem, p_sem) = rest[earlier:-4], rest[-4:]
     region = lax.axis_index("parts")
     first_row = region * row_count
     copies = {}
@@ -45,20 +45,21 @@
             other.start()
             copies[n, k] = (copy, other)
     for n, row in enumerate(rows):
-        for copy in copies[n, 0]:
-            copy.wait()
-        own_t = p_buf[n, 0].T
-        diagonal = dot(own_t, dot(a_buf[n, 0], p_buf[n, 0]).astype(BF16))
-        copies[n, row + 1][0].wait()
-        half = dot(own_t, a_buf[n, row + 1])
-        sums[...] = jnp.zeros_like(sums)
-        for k in range(1, KA):
-            if k == row + 1:
-                continue
+        inner_slots = [k for k in range(1, KA) if k != row + 1]
+        for k in range(KA):
             for copy in copies[n, k]:
                 copy.wait()
+        own_t = p_buf[n, 0].T
+        half = dot(own_t, a_buf[n, row + 1])
+        first = dot(a_buf[n, 0], p_buf[n, 0]).astype(BF16)
+        sums = [None, None]
+        for k in inner_slots:
             side = pcol_ref[cols_ref[k, first_row + row]] % 2
-            sums[side] += dot(a_buf[n, k], p_buf[n, k])
+            product = dot(a_buf[n, k], p_buf[n, k])
+            for c in range(2):
+                part = jnp.where(side == c, product, 0.0)
+                sums[c] = part if sums[c] is None else sums[c] + part
+        diagonal = dot(own_t, first)
         inner = [dot(own_t, sums[c].astype(BF16)) for c in range(2)]
         out_ref, at = (outs[0], (n,)) if len(outs) == 1 else (outs[n], ())
         pack(out_ref, at, [diagonal, inner[0], inner[1], half])
@@ -71,15 +72,15 @@
     smem = pl.BlockSpec(memory_space=pltpu.SMEM)
     vmem = pl.BlockSpec(memory_space=pltpu.VMEM)
     anyw = pl.BlockSpec(memory_space=pl.ANY)
+    hbm = pl.BlockSpec(memory_space=pltpu.HBM)
     return pl.pallas_call(
         functools.partial(face_kernel, rows, row_count, len(earlier)),
         out_shape=[both] if merged else [one, one],
-        in_specs=[smem, smem, anyw, anyw] + [anyw] * len(earlier),
+        in_specs=[smem, smem, hbm, hbm] + [anyw] * len(earlier),
         out_specs=[vmem] * (1 if merged else 2),
         scratch_shapes=[
             pltpu.VMEM((2, KA, width, width), BF16),
             pltpu.VMEM((2, KA, width, width), BF16),
-            pltpu.VMEM((2, width, width), F32),
             pltpu.SemaphoreType.DMA((2, KA)),
             pltpu.SemaphoreType.DMA((2, KA)),
         ],

time: 63.7 us -> 57.2 us (0.90)
  Pallas kernels: 45.4 us -> 38.8 us
    pallas_call x3, Pallas kernels: 20.1 us -> 13.4 us  [face_terms(): pl.pallas_call(functools.partial(face_kernel, rows, row_count, len(earlie...]
  transfers between devices with their start and end apart: 5 -> 5, of which waited for: 0 -> 0; matrix products, arithmetic and copies ran while one was open for 0% -> 0% of each run, Pallas kernels for 52% -> 50%
where the time goes in v2:
time: 57.2 us; the launch traced here: 56.5 us
  Pallas kernels  38.8 us (68%)
  starting transfers between devices  14.3 us (25%)
  local copies, waits for them, and re-layouts  3.34 us (6%)
    pallas_call x1, Pallas kernels, inner_terms(): pl.pallas_call(functools.partial(inner_kernel, row_count, coarse_count, p...  19.3 us
    ppermute x5, starting transfers between devices, per_device(): lax.ppermute(out, 'parts', [(i, (i + by) % regions) for i in range(region...  14.3 us
    pallas_call x3, Pallas kernels, face_terms(): pl.pallas_call(functools.partial(face_kernel, rows, row_count, len(earlie...  13.4 us
    pallas_call x1, Pallas kernels, outer_terms(): pl.pallas_call(functools.partial(outer_kernel, row_count, coarse_count, r...  6.08 us
    unnamed x10, local copies, waits for them, and re-layouts  3.34 us
  transfers between devices with their start and end apart: 5, of which 0 were waited for; matrix products, arithmetic and copies ran while one was open for 0% of the time, Pallas kernels for 50%

profile of v2, /device:TPU:0, one launch (start us, length us, event | category | flops | bytes accessed | tf_op | source)
XLA Modules:
  0.0 56.5 jit_solution(7074999760209827997)
XLA Ops:
  0.0 0.0 copy-start
  0.0 1.9 %copy-done = bf16[32,192,192]{2,1,0:T(8,128)(2,1)S(1)} copy-done((bf16[32,192,192]{2,1,0:T(8,128)(2,1)S(1)}, bf16[32,192,192]{2,1,0:T(8,128)(2,1)}, u32[]{:S(2)}) %copy-start) | copy-done | bytes 2359320
  1.9 0.0 copy-start.2
  1.9 0.8 %copy-done.2 = s32[1024,7]{0,1:T(8,128)S(1)} copy-done((s32[1024,7]{0,1:T(8,128)S(1)}, s32[1024,7]{0,1:T(8,128)}, u32[]{:S(2)}) %copy-start.2) | copy-done | bytes 28696
  2.6 0.0 copy-start.3
  2.7 0.7 %copy-done.3 = s32[1024]{0:T(1024)S(1)} copy-done((s32[1024]{0:T(1024)S(1)}, s32[1024]{0:T(1024)}, u32[]{:S(2)}) %copy-start.3) | copy-done | bytes 4120
  3.3 4.6 %faces_4.1.rest_0_ = bf16[2,6,192,128]{3,2,1,0:T(8,128)(2,1)S(1)} custom-call(s32[7,1024]{1,0:T(8,128)S(1)} %bitcast.3, s32[1024]{0:T(1024)S(1)} %copy-done.3, bf16[32,7,192,192]{3,2,1,0:T(8,128)(2,1)} %a_ref.1, bf16[32,192,192]{2,1,0:T(8,128)(2,1)S(1)} %copy-done), custom_call_target="tpu_custom_call" | custom-call | flops 339738624 | bytes 5000000 | tf_op jit(solution)/shard_map/faces_4/pallas_call | solution.py:76
  7.9 4.1 %collective-permute-start.4 = (bf16[2,6,192,128]{3,2,1,0:T(8,128)(2,1)S(1)}, bf16[2,6,192,128]{3,2,1,0:T(8,128)(2,1)S(1)}, u32[]{:S(2)}, u32[]{:S(2)}) collective-permute-start(bf16[2,6,192,128]{3,2,1,0:T(8,128)(2,1)S(1)} %faces_4.1.rest_0_), channel_id=1, source_target_pairs={{0,16},{1,17},{2,18},{3,19},{4,20},{5,21},{6,22},{7,23},{8,24},{9,... | collective-permute-start | bytes 1769480 | tf_op jit(solution)/shard_map/ppermute | solution.py:201
  12.0 4.4 %faces_2.1 = (bf16[6,192,128]{2,1,0:T(8,128)(2,1)S(1)}, bf16[6,192,128]{2,1,0:T(8,128)(2,1)S(1)}) custom-call(s32[7,1024]{1,0:T(8,128)S(1)} %bitcast.4, s32[1024]{0:T(1024)S(1)} %copy-done.3, bf16[32,7,192,192]{3,2,1,0:T(8,128)(2,1)} %a_ref.1, bf16[32,192,192]{2,1,0:T(8,128)(2,1)S(1)} %copy-done, bf16[2,6,192,128]{3,2,1,0:T(8,128)(2,1)S(1)} %faces_4.1.rest_0_), custom_call_target="tpu_custom_call" | custom-call | flops 339738624 | bytes 5000000 | tf_op jit(solution)/shard_map/faces_2/pallas_call | solution.py:76
  16.4 1.6 %collective-permute-start.2 = (bf16[6,192,128]{2,1,0:T(8,128)(2,1)S(1)}, bf16[6,192,128]{2,1,0:T(8,128)(2,1)S(1)}, u32[]{:S(2)}, u32[]{:S(2)}) collective-permute-start(bf16[6,192,128]{2,1,0:T(8,128)(2,1)S(1)} %get-tuple-element.9.rest_0_), channel_id=1, source_target_pairs={{0,4},{1,5},{2,6},{3,7},{4,8},{5,9},{6,10},{7,11},{8,12},{9,13},{1... | collective-permute-start | bytes 884744 | tf_op jit(solution)/shard_map/ppermute | solution.py:201
  18.0 0.0 copy-start.4
  18.0 3.2 %collective-permute-start.3 = (bf16[6,192,128]{2,1,0:T(8,128)(2,1)S(1)}, bf16[6,192,128]{2,1,0:T(8,128)(2,1)S(1)}, u32[]{:S(2)}, u32[]{:S(2)}) collective-permute-start(bf16[6,192,128]{2,1,0:T(8,128)(2,1)S(1)} %get-tuple-element.10.rest_1_), channel_id=1, source_target_pairs={{0,28},{1,29},{2,30},{3,31},{4,0},{5,1},{6,2},{7,3},{8,4},{9,5},{1... | collective-permute-start | bytes 884744 | tf_op jit(solution)/shard_map/ppermute | solution.py:201
  21.2 4.4 %faces_0.1 = (bf16[6,192,128]{2,1,0:T(8,128)(2,1)S(1)}, bf16[6,192,128]{2,1,0:T(8,128)(2,1)S(1)}) custom-call(s32[7,1024]{1,0:T(8,128)S(1)} %bitcast.5, s32[1024]{0:T(1024)S(1)} %copy-done.3, bf16[32,7,192,192]{3,2,1,0:T(8,128)(2,1)} %a_ref.1, bf16[32,192,192]{2,1,0:T(8,128)(2,1)S(1)} %copy-done, bf16[6,192,128]{2,1,0:T(8,128)(2,1)S(1)} %get-tuple-element.9.rest_0_, ...), custom_call_target="tpu_custom_call" | custom-call | flops 339738624 | bytes 5000000 | tf_op jit(solution)/shard_map/faces_0/pallas_call | solution.py:76
  25.6 0.1 collective-permute-start
  25.7 5.3 %collective-permute-start.1 = (bf16[6,192,128]{2,1,0:T(8,128)(2,1)S(1)}, bf16[6,192,128]{2,1,0:T(8,128)(2,1)S(1)}, u32[]{:S(2)}, u32[]{:S(2)}) collective-permute-start(bf16[6,192,128]{2,1,0:T(8,128)(2,1)S(1)} %get-tuple-element.12), channel_id=1, source_target_pairs={{0,31},{1,0},{2,1},{3,2},{4,3},{5,4},{6,5},{7,6},{8,7},{9,8},{10,9... | collective-permute-start | bytes 884744 | tf_op jit(solution)/shard_map/ppermute | solution.py:201
  31.0 0.0 copy-done.4
  31.0 19.3 %inner.1.rest_6_ = f32[28,192,192]{2,1,0:T(8,128)} custom-call(s32[7,1024]{1,0:T(8,128)S(1)} %bitcast.6, s32[1024]{0:T(1024)S(1)} %copy-done.3, s32[14,64]{1,0:T(8,128)S(1)} %bitcast.7, bf16[32,7,192,192]{3,2,1,0:T(8,128)(2,1)} %a_ref.1, bf16[32,192,192]{2,1,0:T(8,128)(2,1)S(1)} %copy-done), custom_call_target="tpu_custom_call" | custom-call | flops 10305404928 | bytes 60000000 | tf_op jit(solution)/shard_map/inner/pallas_call | solution.py:131
  50.4 0.0 collective-permute-done.2.rest_2_
  50.4 0.0 collective-permute-done.3.rest_3_
  50.4 0.0 collective-permute-done.rest_0_
  50.4 0.0 collective-permute-done.1.rest_1_
  50.4 0.0 collective-permute-done.4.rest_4_
  50.4 0.0 copy-done.1
  50.4 6.1 %outer.1 = f32[28,192,192]{2,1,0:T(8,128)} custom-call(s32[1024]{0:T(1024)S(1)} %copy-done.3, s32[14,64]{1,0:T(8,128)S(1)} %bitcast.8, bf16[6,192,128]{2,1,0:T(8,128)(2,1)S(1)} %collective-permute-done.rest_0_, bf16[6,192,128]{2,1,0:T(8,128)(2,1)S(1)} %collective-permute-done.1.rest_1_, bf16[6,192,128]{2,1,0:T(8,128)(2,1)S(1)} %collective-permute-done.2.rest_2_, ...), custom_call_target="tpu_custom_call" | custom-call | tf_op jit(solution)/shard_map/outer/pallas_call | solution.py:178
  (1 shorter events, 0.0 us)
Async XLA Ops:
  0.0 1.9 %copy-start = (bf16[32,192,192]{2,1,0:T(8,128)(2,1)S(1)}, bf16[32,192,192]{2,1,0:T(8,128)(2,1)}, u32[]{:S(2)}) copy-start(bf16[32,192,192]{2,1,0:T(8,128)(2,1)} %rest_5_.1) | copy-start | bytes 7077892
  1.9 0.8 %copy-start.2 = (s32[1024,7]{0,1:T(8,128)S(1)}, s32[1024,7]{0,1:T(8,128)}, u32[]{:S(2)}) copy-start(s32[1024,7]{0,1:T(8,128)} %param.5) | copy-start | bytes 86020
  2.6 0.7 %copy-start.3 = (s32[1024]{0:T(1024)S(1)}, s32[1024]{0:T(1024)}, u32[]{:S(2)}) copy-start(s32[1024]{0:T(1024)} %pcol_ref.9) | copy-start | bytes 12292
  7.9 42.5 %collective-permute-start.4 = (bf16[2,6,192,128]{3,2,1,0:T(8,128)(2,1)S(1)}, bf16[2,6,192,128]{3,2,1,0:T(8,128)(2,1)S(1)}, u32[]{:S(2)}, u32[]{:S(2)}) collective-permute-start(bf16[2,6,192,128]{3,2,1,0:T(8,128)(2,1)S(1)} %faces_4.1.rest_0_), channel_id=1, source_target_pairs={{0,16},{1,17},{2,18},{3,19},{4,20},{5,21},{6,22},{7,23},{8,24},{9,... | collective-permute-start | bytes 1769480 | tf_op jit(solution)/shard_map/ppermute | solution.py:201
  16.4 33.9 %collective-permute-start.2 = (bf16[6,192,128]{2,1,0:T(8,128)(2,1)S(1)}, bf16[6,192,128]{2,1,0:T(8,128)(2,1)S(1)}, u32[]{:S(2)}, u32[]{:S(2)}) collective-permute-start(bf16[6,192,128]{2,1,0:T(8,128)(2,1)S(1)} %get-tuple-element.9.rest_0_), channel_id=1, source_target_pairs={{0,4},{1,5},{2,6},{3,7},{4,8},{5,9},{6,10},{7,11},{8,12},{9,13},{1... | collective-permute-start | bytes 884744 | tf_op jit(solution)/shard_map/ppermute | solution.py:201
  18.0 13.0 %copy-start.4 = (s32[64,14]{0,1:T(8,128)S(1)}, s32[64,14]{0,1:T(8,128)}, u32[]{:S(2)}) copy-start(s32[64,14]{0,1:T(8,128)} %param.7) | copy-start | bytes 10756
  18.0 32.4 %collective-permute-start.3 = (bf16[6,192,128]{2,1,0:T(8,128)(2,1)S(1)}, bf16[6,192,128]{2,1,0:T(8,128)(2,1)S(1)}, u32[]{:S(2)}, u32[]{:S(2)}) collective-permute-start(bf16[6,192,128]{2,1,0:T(8,128)(2,1)S(1)} %get-tuple-element.10.rest_1_), channel_id=1, source_target_pairs={{0,28},{1,29},{2,30},{3,31},{4,0},{5,1},{6,2},{7,3},{8,4},{9,5},{1... | collective-permute-start | bytes 884744 | tf_op jit(solution)/shard_map/ppermute | solution.py:201
  25.6 24.7 %collective-permute-start = (bf16[6,192,128]{2,1,0:T(8,128)(2,1)S(1)}, bf16[6,192,128]{2,1,0:T(8,128)(2,1)S(1)}, u32[]{:S(2)}, u32[]{:S(2)}) collective-permute-start(bf16[6,192,128]{2,1,0:T(8,128)(2,1)S(1)} %get-tuple-element.11), channel_id=1, source_target_pairs={{0,1},{1,2},{2,3},{3,4},{4,5},{5,6},{6,7},{7,8},{8,9},{9,10},{10,1... | collective-permute-start | bytes 884744 | tf_op jit(solution)/shard_map/ppermute | solution.py:201
  25.7 24.7 %collective-permute-start.1 = (bf16[6,192,128]{2,1,0:T(8,128)(2,1)S(1)}, bf16[6,192,128]{2,1,0:T(8,128)(2,1)S(1)}, u32[]{:S(2)}, u32[]{:S(2)}) collective-permute-start(bf16[6,192,128]{2,1,0:T(8,128)(2,1)S(1)} %get-tuple-element.12), channel_id=1, source_target_pairs={{0,31},{1,0},{2,1},{3,2},{4,3},{5,4},{6,5},{7,6},{8,7},{9,8},{10,9... | collective-permute-start | bytes 884744 | tf_op jit(solution)/shard_map/ppermute | solution.py:201
  31.0 19.4 %copy-start.1 = (bf16[32,192,192]{2,1,0:T(8,128)(2,1)S(1)}, bf16[32,192,192]{2,1,0:T(8,128)(2,1)}, u32[]{:S(2)}) copy-start(bf16[32,192,192]{2,1,0:T(8,128)(2,1)} %rest_5_.1) | copy-start | bytes 7077892
